TPU v7x, 128 devices: a whole 4x4x4 slice. The times are simulated.
128 devices in a mesh: inst: 8 (over z, x_lo), blk: 16 (over y, x_hi, core).
Axes of the slice: x: 4 (x_hi: 2, x_lo: 2; x = x_hi * 2 + x_lo), y: 4, z: 4, core: 2. Of those that a mesh axis runs over, the one named last changes fastest.
Arguments:
- psi_start: float32 [8, 6, 128, 8192], P('inst', None, 'blk'), may hold values from -6 to 6
- coupling: float32 [8, 6, 6], P('inst'), may hold values from -2.5 to 2.5
- center: float32 [8, 128, 8192], P('inst', 'blk'), may hold values from 4 to 8
- spread: float32 [8, 128, 8192], P('inst', 'blk'), may hold values from 0.2 to 1
- source: float32 [8, 6, 128, 8192], P('inst', None, 'blk'), may hold values from -6 to 6
- wall_geo: float32 [8, 18, 32768], P('inst', None, 'blk'), may hold values from -6 to 6
- wall_cell: int32 [32768], P('blk'), may hold values from 0 to 65535
- wall_dest: int32 [32768, 1], P('blk'), may hold values from 0 to 15; in each aligned block of 2048 rows (0 to 2047, 2048 to 4095, ...) at most 256 rows name the same one
- wall_node: int32 [32768], P('blk'), may hold values from 0 to 4095
Outputs:
- psi_out: float32 [8, 6, 128, 8192], P('inst', None, 'blk')
- sensitivity: float32 [3, 65536], P(None, 'blk')
Inputs may be any that keep to these rules, and one draw needn't show every extreme that they name: `wall_dest`: among the 2048 wall faces of one grid block at most 256 go to one owner.
All inputs are finite; a program needn't handle non-finite values.
Results may differ from a plain program's by a relative error of at most 0.0001.
Values sent between devices are 32-bit elements; how exact they have to be, the bound alone decides.
No kernel may reach another device: no remote copies, remote signals or barrier semaphores. Data moves between devices by JAX's collectives and lax.ppermute only.
A program may use at most 192 MiB of HBM per device.

v0:
```python
import jax
import jax.numpy as jnp
from jax import lax
from jax.sharding import PartitionSpec as P

CAP = 256
NODE_DEV = 4096
ITERS = 2


def extended(shard, sides, width):
    for axis, dim in sides:
        devices, length = (lax.axis_size(axis), shard.shape[dim])
        up = [(i, (i + 1) % devices) for i in range(devices)]
        down = [(j, i) for i, j in up]
        last = lax.slice_in_dim(shard, length - width, length, axis=dim)
        leading = lax.slice_in_dim(shard, 0, width, axis=dim)
        before = lax.ppermute(last, axis, up)
        after = lax.ppermute(leading, axis, down)
        shard = jnp.concatenate([before, shard, after], axis=dim)
    return shard


def spectral_matrix(count):
    index = jnp.arange(count, dtype=jnp.int32)
    offset = index[:, None] - index[None, :]
    parity = (offset % 2).astype(jnp.float32)
    same = offset == 0
    angle = jnp.pi * offset.astype(jnp.float32) / count
    safe_angle = jnp.where(same, 1.0, angle)
    values = 0.5 * (1.0 - 2.0 * parity) / jnp.sin(safe_angle)
    return jnp.where(same, 0.0, values)


def spectral_source(psi, spec_mat):
    own_count = psi.shape[0]
    own_start = lax.axis_index("inst") * own_count
    piece = lax.all_gather(psi, "inst", axis=0, tiled=True)
    part_mat = lax.dynamic_slice(spec_mat, (0, own_start), (piece.shape[0], own_count))
    total = jnp.einsum("ji,jfxy->ifxy", part_mat, piece, precision=lax.Precision.HIGHEST)
    return 0.5 * total


def sweep(psi, coupling, center, spread, source, spec_mat):
    mixed = jnp.einsum("igf,igxy->ifxy", coupling, psi, precision=lax.Precision.HIGHEST)
    weighted = spread[:, None] * mixed
    rimmed = extended(weighted, (("blk", 2),), 1)
    beside = rimmed[:, :, 2:, :] + rimmed[:, :, :-2, :]
    padded = jnp.pad(weighted, ((0, 0), (0, 0), (0, 0), (1, 1)))
    beside = beside + padded[..., 2:] + padded[..., :-2]
    spectral = spectral_source(psi, spec_mat)
    update = center[:, None] * psi - beside + spectral - source
    return psi - (0.6 / center)[:, None] * update


def wall_partials(psi, wall_geo, wall_cell):
    inst_count, fields = (psi.shape[0], psi.shape[1])
    flat = psi.reshape(inst_count, fields, -1)
    picked = flat[:, :, wall_cell]
    geometry = wall_geo.reshape(inst_count, 3, fields, -1)
    partial_value = jnp.einsum("ikfe,ife->ike", geometry, picked, precision=lax.Precision.HIGHEST)
    return partial_value.reshape(inst_count * 3, -1)


def owner_slots(wall_dest, owners):
    dest = wall_dest[:, 0]
    onehot = (dest[:, None] == jnp.arange(owners, dtype=jnp.int32)[None, :]).astype(jnp.int32)
    before = jnp.cumsum(onehot, axis=0) - onehot
    rank = jnp.sum(before * onehot, axis=1)
    return (dest, rank)


def pack_slots(partial_value, dest, rank, wall_node, owners):
    rows = partial_value.shape[0]
    value_buf = jnp.zeros((rows, owners, CAP), jnp.float32).at[:, dest, rank].set(partial_value)
    node_buf = jnp.zeros((1, owners, CAP), jnp.int32).at[0, dest, rank].set(wall_node)
    return (value_buf, node_buf)


def unpack_slots(got_values, got_nodes):
    rows = got_values.shape[0]
    summed = jax.ops.segment_sum(
        got_values.reshape(rows, -1).T, got_nodes.reshape(-1), num_segments=NODE_DEV
    )
    return jnp.sum(summed.T.reshape(rows // 3, 3, NODE_DEV), axis=0)


def local(psi_start, coupling, center, spread, source, wall_geo, wall_cell, wall_dest, wall_node):
    owners = lax.axis_size("blk")
    spec_mat = spectral_matrix(psi_start.shape[0] * lax.axis_size("inst"))
    dest, rank = owner_slots(wall_dest, owners)
    sens_local = jnp.zeros((3, NODE_DEV), jnp.float32)
    psi = psi_start
    for step in range(ITERS):
        psi = sweep(psi, coupling, center, spread, source, spec_mat)
        partial_value = wall_partials(psi, wall_geo, wall_cell)
        value_buf, node_buf = pack_slots(partial_value, dest, rank, wall_node, owners)
        got_values, got_nodes = (
            lax.all_to_all(value_buf, "blk", split_axis=1, concat_axis=1, tiled=True),
            lax.all_to_all(node_buf, "blk", split_axis=1, concat_axis=1, tiled=True),
        )
        sens_local = sens_local + unpack_slots(got_values, got_nodes)
    sensitivity = lax.psum(sens_local, "inst")
    return (psi, sensitivity)


def solution(mesh):
    placed = (
        P("inst", None, "blk", None),
        P("inst", None, None),
        P("inst", "blk", None),
        P("inst", "blk", None),
        P("inst", None, "blk", None),
        P("inst", None, "blk"),
        P("blk"),
        P("blk", None),
        P("blk"),
    )
    return jax.shard_map(
        local,
        mesh=mesh,
        in_specs=placed,
        out_specs=(P("inst", None, "blk", None), P(None, "blk")),
        check_vma=False,
    )
```

profile of v0, /device:TPU:12, one launch (start us, length us, event | category | flops | bytes accessed | tf_op | source)
XLA Modules:
  0.0 807.7 jit_solution(17933240960903875595)
XLA Ops:
  7.2 0.7 all-gather.3.cloned.1.call-update
  8.0 0.6 copy-done.1
  8.6 4.3 fusion.4
  12.9 1.4 copy-done.3
  14.3 0.6 collective-permute-start.1
  15.1 244.9 %all-gather.3.cloned.1.call-done = f32[8,6,8,8192]{3,2,1,0:T(8,128)} async-done(((f32[1,6,8,8192]{3,2,1,0:T(8,128)}), f32[8,6,8,8192]{3,2,1,0:T(8,128)}) %all-gather.3.cloned.1.call-update) | async-done | bytes 12582928 | tf_op jit(solution)/shard_map/all_gather | solution.py:38
  260.0 22.3 %fusion.2 = f32[1,6,8,8192]{3,0,2,1:T(1,128)S(1)} fusion(f32[8,6,8,8192]{3,2,1,0:T(8,128)} %all-gather.3.cloned.1.call-done, f32[8,8]{0,1:T(8,128)S(1)} %fusion.42, s32[]{:T(128)S(6)} %select_n.45), kind=kOutput, calls=%fused_computation.9 | convolution fusion | flops 37748736 | bytes 14156292 | tf_op jit(solution)/shard_map/ji,jfxy->ifxy/dot_general | solution.py:40
  282.4 5.1 copy_subtract_fusion
  287.5 2.1 copy.51
  289.6 4.5 reduce-window.6
  294.1 0.4 slice_reduce_fusion
  294.6 0.2 reduce-window.9
  294.7 0.1 broadcast_add_fusion
  295.0 0.1 multiply_reduce_fusion
  295.1 0.1 and_reduce_fusion.1
  295.2 8.8 %scatter_custom_fusion.2 = s32[4096]{0:T(1024)} fusion(s32[2048]{0:T(1024)S(1)} %broadcast_select_fusion.1, s32[2048]{0:T(1024)} %param.17, s32[]{:T(128)} %constant.18.clone.1), kind=kCustom, calls=%fused_computation.69 | custom fusion | bytes 16896
  304.0 8.2 %all-to-all-start = ((s32[1,16,256]{2,0,1:T(1,128)}), s32[1,16,256]{2,0,1:T(1,128)S(1)}, u32[]{:S(2)}, u32[]{:S(2)}) async-start(s32[1,16,256]{2,0,1:T(1,128)} %bitcast.24), calls=%async_computation | async-start | bytes 32768 | tf_op jit(solution)/shard_map/all_to_all | solution.py:100
  312.1 0.3 reduce.7
  312.6 3.1 copy.70
  315.8 0.1 and_reduce_fusion
  316.0 2.1 fusion.5
  318.1 1.3 copy-done.5
  319.4 0.7 fusion.53
  320.1 0.3 collective-permute-start.2
  320.4 0.2 collective-permute-start.3
  320.6 17.3 %copy.53 = f32[6,65536]{0,1:T(8,128)} copy(f32[6,65536]{1,0:T(8,128)S(1)} %bitcast.101) | data formatting | bytes 3145728 | tf_op jit(solution)/shard_map/reshape | solution.py:58
  337.9 18.2 %gather_fusion = f32[2048,6]{1,0:T(8,128)} fusion(f32[6,65536]{0,1:T(8,128)} %copy.53, s32[2048]{0:T(1024)S(1)} %fusion.33), kind=kCustom, calls=%fused_computation | custom fusion | bytes 106496 | tf_op jit(solution)/shard_map/gather | solution.py:59
  356.1 16.6 %fusion.55 = f32[2048,1,3]{2,1,0:T(1,128)} fusion(f32[6,2048,1]{0,2,1:T(1,128)} %bitcast.120, f32[3,6,2048]{1,0,2:T(4,128)} %copy.70), kind=kOutput, calls=%fused_computation.97 | convolution fusion | flops 442368 | bytes 221184 | tf_op jit(solution)/shard_map/ikfe,ife->ike/dot_general | solution.py:61
  372.7 7.4 scatter_custom_fusion.3
  380.1 2.8 copy.54
  382.9 161.9 %all-gather.5.cloned.1.call-done = f32[8,6,8,8192]{3,2,1,0:T(8,128)} async-done(((f32[1,6,8,8192]{3,2,1,0:T(8,128)}), f32[8,6,8,8192]{3,2,1,0:T(8,128)}) %all-gather.5.cloned.1.call-update) | async-done | bytes 12582928 | tf_op jit(solution)/shard_map/all_gather | solution.py:38
  544.8 22.5 %fusion = f32[1,6,8,8192]{3,0,2,1:T(1,128)S(1)} fusion(f32[8,6,8,8192]{3,2,1,0:T(8,128)} %all-gather.5.cloned.1.call-done, f32[8,8]{0,1:T(8,128)S(1)} %fusion.42, s32[]{:T(128)S(6)} %select_n.45), kind=kOutput, calls=%fused_computation.7 | convolution fusion | flops 37748736 | bytes 14156292 | tf_op jit(solution)/shard_map/ji,jfxy->ifxy/dot_general | solution.py:40
  567.3 5.0 fusion.8
  572.3 16.5 %copy.56 = f32[6,65536]{0,1:T(8,128)} copy(f32[6,65536]{1,0:T(8,128)} %bitcast.102) | data formatting | bytes 3145728 | tf_op jit(solution)/shard_map/reshape | solution.py:58
  588.8 16.0 %gather_fusion.1 = f32[2048,6]{1,0:T(8,128)S(1)} fusion(f32[6,65536]{0,1:T(8,128)} %copy.56, s32[2048]{0:T(1024)S(1)} %fusion.33), kind=kCustom, calls=%fused_computation.1 | custom fusion | bytes 106496 | tf_op jit(solution)/shard_map/gather | solution.py:59
  604.8 7.3 all-to-all-start.1
  612.1 16.3 %fusion.56 = f32[2048,1,3]{2,1,0:T(1,128)} fusion(f32[6,2048,1]{0,2,1:T(1,128)S(1)} %bitcast.119, f32[3,6,2048]{1,0,2:T(4,128)} %copy.70), kind=kOutput, calls=%fused_computation.98 | convolution fusion | flops 442368 | bytes 221184 | tf_op jit(solution)/shard_map/ikfe,ife->ike/dot_general | solution.py:61
  628.3 6.5 scatter_custom_fusion.4
  634.8 1.3 copy.57
  636.0 7.6 all-to-all-start.2
  643.6 1.9 copy.55
  645.6 28.8 %scatter_custom_fusion = f32[4096,3]{1,0:T(8,128)} fusion(s32[4096]{0:T(1024)S(1)} %bitcast.117, f32[4096,3]{1,0:T(8,128)} %copy.55, f32[]{:T(128)} %constant.17.clone.1), kind=kCustom, calls=%fused_computation.47 | custom fusion | flops 12288 | bytes 49664 | tf_op jit(solution)/shard_map/scatter-add | solution.py:82
  674.4 2.1 copy.59
  676.4 2.0 copy.58
  678.4 28.7 %scatter_custom_fusion.1 = f32[4096,3]{1,0:T(8,128)} fusion(s32[4096]{0:T(1024)S(1)} %bitcast.118, f32[4096,3]{1,0:T(8,128)} %copy.58, f32[]{:T(128)} %constant.17.clone.1), kind=kCustom, calls=%fused_computation.45 | custom fusion | flops 12288 | bytes 49664 | tf_op jit(solution)/shard_map/scatter-add | solution.py:82
  707.2 3.1 add_bitcast_fusion
  710.3 89.1 %psum.7 = f32[3,4096]{0,1:T(8,128)S(1)} all-reduce(f32[3,4096]{0,1:T(8,128)} %add_bitcast_fusion), channel_id=1, replica_groups=mesh['inst'=8,'blk'=16] {'inst'}, use_global_device_ids=true, to_apply=%region_8.9 | all-reduce | flops 12288 | bytes 98304 | tf_op jit(solution)/shard_map/psum | solution.py:103
  799.4 1.2 copy.60
  (60 shorter events, 0.6 us)
Async XLA Ops:
  7.2 1.4 copy-start.1
  7.2 252.8 %all-gather.3.cloned.1.call-start = ((), (), s32[]{:S(2)}) async-start(), calls=%async_computation.3 | async-start | bytes 14155776 | tf_op jit(solution)/shard_map/all_gather | solution.py:38
  7.9 536.9 %all-gather.5.cloned.1.call-start = ((), (), s32[]{:S(2)}) async-start(), calls=%async_computation.4 | async-start | bytes 14155776 | tf_op jit(solution)/shard_map/all_gather | solution.py:38
  8.6 6.5 copy-start.10
  12.8 1.4 copy-start.3
  14.2 268.1 %collective-permute-start = (f32[1,6,1,8192]{3,1,2,0:T(8,128)S(1)}, f32[1,6,1,8192]{3,1,2,0:T(8,128)S(1)}, u32[]{:S(2)}, u32[]{:S(2)}) collective-permute-start(f32[1,6,1,8192]{3,1,2,0:T(8,128)S(1)} %get-tuple-element.12), channel_id=1, source_target_pairs={{1,0},{2,1},{3,2},{4,3},{5,4},{6,5},{7,6},{8,7},{9,8},{10,9},{11,1... | collective-permute-start | bytes 589832 | tf_op jit(solution)/shard_map/ppermute | solution.py:19
  14.3 268.0 %collective-permute-start.1 = (f32[1,6,1,8192]{3,1,2,0:T(8,128)S(1)}, f32[1,6,1,8192]{3,1,2,0:T(8,128)S(1)}, u32[]{:S(2)}, u32[]{:S(2)}) collective-permute-start(f32[1,6,1,8192]{3,1,2,0:T(8,128)S(1)} %get-tuple-element.13), channel_id=1, source_target_pairs={{0,1},{1,2},{2,3},{3,4},{4,5},{5,6},{6,7},{7,8},{8,9},{9,10},{10,1... | collective-permute-start | bytes 589832 | tf_op jit(solution)/shard_map/ppermute | solution.py:18
  260.0 22.3 %copy-start.2 = (f32[1,6,8,8192]{3,2,1,0:T(8,128)S(1)}, f32[1,6,8,8192]{3,2,1,0:T(8,128)}, u32[]{:S(2)}) copy-start(f32[1,6,8,8192]{3,2,1,0:T(8,128)} %param.9) | copy-start | bytes 4718596
  260.0 22.4 %copy-start.4 = (f32[1,6,8,8192]{3,1,2,0:T(8,128)S(1)}, f32[1,6,8,8192]{3,1,2,0:T(8,128)}, u32[]{:S(2)}) copy-start(f32[1,6,8,8192]{3,1,2,0:T(8,128)} %copy-done.3) | copy-start | bytes 4718596
  260.0 22.4 %copy-start.8 = (f32[1,6,8,8192]{3,2,1,0:T(8,128)S(1)}, f32[1,6,8,8192]{3,2,1,0:T(8,128)}, u32[]{:S(2)}) copy-start(f32[1,6,8,8192]{3,2,1,0:T(8,128)} %param.13) | copy-start | bytes 4718596
  287.5 2.1 copy-start.13
  289.5 5.4 copy-start.16
  289.5 5.5 copy-start.19
  289.5 22.6 %copy-start.12 = (f32[1,18,2048]{2,0,1:T(1,128)S(1)}, f32[1,18,2048]{2,0,1:T(1,128)}, u32[]{:S(2)}) copy-start(f32[1,18,2048]{2,0,1:T(1,128)} %param.14) | copy-start | bytes 442372
  304.0 300.8 %all-to-all-start = ((s32[1,16,256]{2,0,1:T(1,128)}), s32[1,16,256]{2,0,1:T(1,128)S(1)}, u32[]{:S(2)}, u32[]{:S(2)}) async-start(s32[1,16,256]{2,0,1:T(1,128)} %bitcast.24), calls=%async_computation | async-start | bytes 32768 | tf_op jit(solution)/shard_map/all_to_all | solution.py:100
  312.5 3.2 copy-start.18
  312.5 3.3 copy-start.17
  312.6 3.4 copy-start.15
  312.6 3.4 copy-start.11
  312.6 3.4 copy-start.14
  318.1 1.3 copy-start.5
  320.1 247.2 %collective-permute-start.2 = (f32[1,6,1,8192]{3,1,2,0:T(8,128)}, f32[1,6,1,8192]{3,1,2,0:T(8,128)S(1)}, u32[]{:S(2)}, u32[]{:S(2)}) collective-permute-start(f32[1,6,1,8192]{3,1,2,0:T(8,128)} %get-tuple-element.10), channel_id=1, source_target_pairs={{1,0},{2,1},{3,2},{4,3},{5,4},{6,5},{7,6},{8,7},{9,8},{10,9},{11,1... | collective-permute-start | bytes 589832 | tf_op jit(solution)/shard_map/ppermute | solution.py:19
  320.4 246.8 %collective-permute-start.3 = (f32[1,6,1,8192]{3,1,2,0:T(8,128)S(1)}, f32[1,6,1,8192]{3,1,2,0:T(8,128)S(1)}, u32[]{:S(2)}, u32[]{:S(2)}) collective-permute-start(f32[1,6,1,8192]{3,1,2,0:T(8,128)S(1)} %get-tuple-element.11), channel_id=1, source_target_pairs={{0,1},{1,2},{2,3},{3,4},{4,5},{5,6},{6,7},{7,8},{8,9},{9,10},{10,1... | collective-permute-start | bytes 589832 | tf_op jit(solution)/shard_map/ppermute | solution.py:18
  544.8 22.5 %copy-start.6 = (f32[1,6,8,8192]{3,1,2,0:T(8,128)S(1)}, f32[1,6,8,8192]{3,1,2,0:T(8,128)}, u32[]{:S(2)}) copy-start(f32[1,6,8,8192]{3,1,2,0:T(8,128)} %copy-done.5) | copy-start | bytes 4718596
  544.8 22.5 %copy-start.9 = (f32[1,6,8,8192]{3,2,1,0:T(8,128)S(1)}, f32[1,6,8,8192]{3,2,1,0:T(8,128)}, u32[]{:S(2)}) copy-start(f32[1,6,8,8192]{3,2,1,0:T(8,128)} %param.13) | copy-start | bytes 4718596
  604.8 31.2 %all-to-all-start.1 = ((f32[3,16,256]{2,0,1:T(4,128)}), f32[3,16,256]{2,0,1:T(4,128)S(1)}, u32[]{:S(2)}, u32[]{:S(2)}) async-start(f32[3,16,256]{2,0,1:T(4,128)} %copy.54), calls=%async_computation.1 | async-start | bytes 131072 | tf_op jit(solution)/shard_map/all_to_all | solution.py:99
  636.0 40.4 %all-to-all-start.2 = ((f32[3,16,256]{2,0,1:T(4,128)}), f32[3,16,256]{2,0,1:T(4,128)S(1)}, u32[]{:S(2)}, u32[]{:S(2)}) async-start(f32[3,16,256]{2,0,1:T(4,128)} %copy.57), calls=%async_computation.2 | async-start | bytes 131072 | tf_op jit(solution)/shard_map/all_to_all | solution.py:99
  643.6 30.8 %copy-start = (f32[1,6,8,8192]{3,1,2,0:T(8,128)S(1)}, f32[1,6,8,8192]{3,1,2,0:T(8,128)}, u32[]{:S(2)}) copy-start(f32[1,6,8,8192]{3,1,2,0:T(8,128)} %fusion.8) | copy-start | bytes 4718596
  676.4 30.7 %copy-start.7 = (f32[4096,3]{1,0:T(8,128)S(1)}, f32[4096,3]{1,0:T(8,128)}, u32[]{:S(2)}) copy-start(f32[4096,3]{1,0:T(8,128)} %scatter_custom_fusion) | copy-start | bytes 147460
Sparse Core Ops, SparseCore 0:
  9.7 250.3 all-gather.2
  289.7 255.0 all-gather.4
where the time goes:
time: 812 us; the launch traced here: 808 us
  waiting for transfers between devices  408 us (50%)
  local copies, waits for them, and re-layouts  112 us (14%)
  blocking collectives  89.1 us (11%)
  matrix products  83.9 us (10%)
  other arithmetic  76.5 us (9%)
  starting transfers between devices  24.3 us (3%)
  between operations  14.7 us (2%)
    all_gather x2, waiting for transfers between devices, spectral_source(): piece = lax.all_gather(psi, 'inst', axis=0, tiled=True)  407 us
    psum x1, blocking collectives, local(): sensitivity = lax.psum(sens_local, 'inst')  89.1 us
    scatter-add x2, other arithmetic, unpack_slots(): jax.ops.segment_sum(got_values.reshape(rows, -1).T, got_nodes.reshape(-1)...  57.5 us
    dot_general x2, matrix products, spectral_source(): jnp.einsum('ji,jfxy->ifxy', part_mat, piece, precision=lax.Precision.HIGH...  44.8 us
    gather x2, local copies, waits for them, and re-layouts, wall_partials(): picked = flat[:, :, wall_cell]  34.2 us
    reshape x2, local copies, waits for them, and re-layouts, wall_partials(): flat = psi.reshape(inst_count, fields, -1)  33.8 us
    dot_general x2, matrix products, wall_partials(): jnp.einsum('ikfe,ife->ike', geometry, picked, precision=lax.Precision.HIG...  32.8 us
    unnamed x45, local copies, waits for them, and re-layouts  29.3 us
  transfers between devices with their start and end apart: 9, of which 2 were waited for; matrix products, arithmetic and copies ran while one was open for 28% of the time, Pallas kernels for 0%

commit v1 on v0

--- a/solution.py
+++ b/solution.py
@@ -100,7 +100,7 @@
             lax.all_to_all(node_buf, "blk", split_axis=1, concat_axis=1, tiled=True),
         )
         sens_local = sens_local + unpack_slots(got_values, got_nodes)
-    sensitivity = lax.psum(sens_local, "inst")
+    sensitivity = jnp.sum(lax.all_gather(sens_local, "inst"), axis=0)
     return (psi, sensitivity)
 
 

time: 812 us -> 755 us (0.930)
  blocking collectives: 89.1 us -> 30.2 us
    psum x1 -> x0, blocking collectives: 89.1 us -> none  [local(): sensitivity = lax.psum(sens_local, 'inst')]
    all_gather x0 -> x1, blocking collectives: none -> 30.2 us  [local(): sensitivity = jnp.sum(lax.all_gather(sens_local, 'inst'), axis=0)]
  transfers between devices with their start and end apart: 9 -> 9, of which waited for: 2 -> 2; matrix products, arithmetic and copies ran while one was open for 28% -> 30% of each run, Pallas kernels for 0% -> 0%
where the time goes in v1:
time: 755 us; the launch traced here: 750 us
  waiting for transfers between devices  408 us (54%)
  local copies, waits for them, and re-layouts  113 us (15%)
  matrix products  83.9 us (11%)
  other arithmetic  77.2 us (10%)
  blocking collectives  30.2 us (4%)
  starting transfers between devices  24.3 us (3%)
  between operations  14.7 us (2%)
    all_gather x2, waiting for transfers between devices, spectral_source(): piece = lax.all_gather(psi, 'inst', axis=0, tiled=True)  407 us
    scatter-add x2, other arithmetic, unpack_slots(): jax.ops.segment_sum(got_values.reshape(rows, -1).T, got_nodes.reshape(-1)...  57.5 us
    dot_general x2, matrix products, spectral_source(): jnp.einsum('ji,jfxy->ifxy', part_mat, piece, precision=lax.Precision.HIGH...  44.8 us
    gather x2, local copies, waits for them, and re-layouts, wall_partials(): picked = flat[:, :, wall_cell]  34.2 us
    reshape x2, local copies, waits for them, and re-layouts, wall_partials(): flat = psi.reshape(inst_count, fields, -1)  33.8 us
    dot_general x2, matrix products, wall_partials(): jnp.einsum('ikfe,ife->ike', geometry, picked, precision=lax.Precision.HIG...  32.8 us
    unnamed x45, local copies, waits for them, and re-layouts  30.2 us
    all_gather x1, blocking collectives, local(): sensitivity = jnp.sum(lax.all_gather(sens_local, 'inst'), axis=0)  30.2 us
  transfers between devices with their start and end apart: 9, of which 2 were waited for; matrix products, arithmetic and copies ran while one was open for 30% of the time, Pallas kernels for 0%

profile of v1, /device:TPU:12, one launch (start us, length us, event | category | flops | bytes accessed | tf_op | source)
XLA Modules:
  0.0 750.5 jit_solution(13407548063474160628)
XLA Ops:
  7.2 0.7 all-gather.5.cloned.1.call-update
  8.0 0.6 copy-done.1
  8.6 4.3 fusion.4
  12.9 1.4 copy-done.3
  14.3 0.6 collective-permute-start.1
  15.1 244.9 %all-gather.5.cloned.1.call-done = f32[8,6,8,8192]{3,2,1,0:T(8,128)} async-done(((f32[1,6,8,8192]{3,2,1,0:T(8,128)}), f32[8,6,8,8192]{3,2,1,0:T(8,128)}) %all-gather.5.cloned.1.call-update) | async-done | bytes 12582928 | tf_op jit(solution)/shard_map/all_gather | solution.py:38
  260.0 22.3 %fusion.2 = f32[1,6,8,8192]{3,0,2,1:T(1,128)S(1)} fusion(f32[8,6,8,8192]{3,2,1,0:T(8,128)} %all-gather.5.cloned.1.call-done, f32[8,8]{0,1:T(8,128)S(1)} %fusion.42, s32[]{:T(128)S(6)} %select_n.45), kind=kOutput, calls=%fused_computation.9 | convolution fusion | flops 37748736 | bytes 14156292 | tf_op jit(solution)/shard_map/ji,jfxy->ifxy/dot_general | solution.py:40
  282.4 5.1 copy_subtract_fusion
  287.5 2.1 copy.51
  289.6 4.5 reduce-window.6
  294.1 0.4 slice_reduce_fusion
  294.6 0.2 reduce-window.9
  294.7 0.1 broadcast_add_fusion
  295.1 0.1 and_reduce_fusion.1
  295.2 8.8 %scatter_custom_fusion.2 = s32[4096]{0:T(1024)} fusion(s32[2048]{0:T(1024)S(1)} %broadcast_select_fusion.1, s32[2048]{0:T(1024)} %param.17, s32[]{:T(128)} %constant.18.clone.1), kind=kCustom, calls=%fused_computation.69 | custom fusion | bytes 16896
  304.0 8.2 %all-to-all-start = ((s32[1,16,256]{2,0,1:T(1,128)}), s32[1,16,256]{2,0,1:T(1,128)S(1)}, u32[]{:S(2)}, u32[]{:S(2)}) async-start(s32[1,16,256]{2,0,1:T(1,128)} %bitcast.24), calls=%async_computation | async-start | bytes 32768 | tf_op jit(solution)/shard_map/all_to_all | solution.py:100
  312.1 0.3 reduce.8
  312.6 3.1 copy.72
  315.8 0.1 and_reduce_fusion
  316.0 2.1 fusion.5
  318.1 1.3 copy-done.5
  319.4 0.7 fusion.53
  320.1 0.3 collective-permute-start.2
  320.4 0.2 collective-permute-start.3
  320.6 17.3 %copy.53 = f32[6,65536]{0,1:T(8,128)} copy(f32[6,65536]{1,0:T(8,128)S(1)} %bitcast.103) | data formatting | bytes 3145728 | tf_op jit(solution)/shard_map/reshape | solution.py:58
  337.9 18.2 %gather_fusion = f32[2048,6]{1,0:T(8,128)} fusion(f32[6,65536]{0,1:T(8,128)} %copy.53, s32[2048]{0:T(1024)S(1)} %fusion.33), kind=kCustom, calls=%fused_computation | custom fusion | bytes 106496 | tf_op jit(solution)/shard_map/gather | solution.py:59
  356.1 16.6 %fusion.55 = f32[2048,1,3]{2,1,0:T(1,128)} fusion(f32[6,2048,1]{0,2,1:T(1,128)} %bitcast.122, f32[3,6,2048]{1,0,2:T(4,128)} %copy.72), kind=kOutput, calls=%fused_computation.97 | convolution fusion | flops 442368 | bytes 221184 | tf_op jit(solution)/shard_map/ikfe,ife->ike/dot_general | solution.py:61
  372.7 7.4 scatter_custom_fusion.3
  380.1 2.8 copy.54
  382.9 161.9 %all-gather.7.cloned.1.call-done = f32[8,6,8,8192]{3,2,1,0:T(8,128)} async-done(((f32[1,6,8,8192]{3,2,1,0:T(8,128)}), f32[8,6,8,8192]{3,2,1,0:T(8,128)}) %all-gather.7.cloned.1.call-update) | async-done | bytes 12582928 | tf_op jit(solution)/shard_map/all_gather | solution.py:38
  544.8 22.5 %fusion = f32[1,6,8,8192]{3,0,2,1:T(1,128)S(1)} fusion(f32[8,6,8,8192]{3,2,1,0:T(8,128)} %all-gather.7.cloned.1.call-done, f32[8,8]{0,1:T(8,128)S(1)} %fusion.42, s32[]{:T(128)S(6)} %select_n.45), kind=kOutput, calls=%fused_computation.7 | convolution fusion | flops 37748736 | bytes 14156292 | tf_op jit(solution)/shard_map/ji,jfxy->ifxy/dot_general | solution.py:40
  567.3 5.0 fusion.8
  572.3 16.5 %copy.56 = f32[6,65536]{0,1:T(8,128)} copy(f32[6,65536]{1,0:T(8,128)} %bitcast.104) | data formatting | bytes 3145728 | tf_op jit(solution)/shard_map/reshape | solution.py:58
  588.8 16.0 %gather_fusion.1 = f32[2048,6]{1,0:T(8,128)S(1)} fusion(f32[6,65536]{0,1:T(8,128)} %copy.56, s32[2048]{0:T(1024)S(1)} %fusion.33), kind=kCustom, calls=%fused_computation.1 | custom fusion | bytes 106496 | tf_op jit(solution)/shard_map/gather | solution.py:59
  604.8 7.3 all-to-all-start.1
  612.1 16.3 %fusion.56 = f32[2048,1,3]{2,1,0:T(1,128)} fusion(f32[6,2048,1]{0,2,1:T(1,128)S(1)} %bitcast.121, f32[3,6,2048]{1,0,2:T(4,128)} %copy.72), kind=kOutput, calls=%fused_computation.98 | convolution fusion | flops 442368 | bytes 221184 | tf_op jit(solution)/shard_map/ikfe,ife->ike/dot_general | solution.py:61
  628.3 6.5 scatter_custom_fusion.4
  634.8 1.3 copy.57
  636.0 7.6 %all-to-all-start.2 = ((f32[3,16,256]{2,0,1:T(4,128)}), f32[3,16,256]{2,0,1:T(4,128)S(1)}, u32[]{:S(2)}, u32[]{:S(2)}) async-start(f32[3,16,256]{2,0,1:T(4,128)} %copy.57), calls=%async_computation.2 | async-start | bytes 131072 | tf_op jit(solution)/shard_map/all_to_all | solution.py:99
  643.6 1.9 copy.55
  645.6 28.8 %scatter_custom_fusion = f32[4096,3]{1,0:T(8,128)} fusion(s32[4096]{0:T(1024)S(1)} %bitcast.119, f32[4096,3]{1,0:T(8,128)} %copy.55, f32[]{:T(128)} %constant.17.clone.1), kind=kCustom, calls=%fused_computation.47 | custom fusion | flops 12288 | bytes 49664 | tf_op jit(solution)/shard_map/scatter-add | solution.py:82
  674.4 2.1 copy.61
  676.4 2.0 copy.58
  678.4 28.7 %scatter_custom_fusion.1 = f32[4096,3]{1,0:T(8,128)} fusion(s32[4096]{0:T(1024)S(1)} %bitcast.120, f32[4096,3]{1,0:T(8,128)} %copy.58, f32[]{:T(128)} %constant.17.clone.1), kind=kCustom, calls=%fused_computation.45 | custom fusion | flops 12288 | bytes 49664 | tf_op jit(solution)/shard_map/scatter-add | solution.py:82
  707.2 3.1 add_bitcast_fusion
  710.3 2.2 copy.59
  712.5 30.2 %all-gather.1 = f32[8,3,4096]{2,1,0:T(4,128)S(1)} all-gather(f32[1,3,4096]{2,1,0:T(4,128)S(1)} %copy.59), channel_id=2, replica_groups=mesh['inst'=8,'blk'=16] {'inst'}, dimensions={0}, use_global_device_ids=true | all-gather | bytes 442368 | tf_op jit(solution)/shard_map/all_gather | solution.py:103
  742.7 0.7 reduce_sum.23
  (61 shorter events, 0.7 us)
Async XLA Ops:
  7.2 1.4 copy-start.1
  7.2 252.8 %all-gather.5.cloned.1.call-start = ((), (), s32[]{:S(2)}) async-start(), calls=%async_computation.3 | async-start | bytes 14155776 | tf_op jit(solution)/shard_map/all_gather | solution.py:38
  7.9 536.9 %all-gather.7.cloned.1.call-start = ((), (), s32[]{:S(2)}) async-start(), calls=%async_computation.4 | async-start | bytes 14155776 | tf_op jit(solution)/shard_map/all_gather | solution.py:38
  8.6 6.5 copy-start.10
  12.8 1.4 copy-start.3
  14.2 268.1 %collective-permute-start = (f32[1,6,1,8192]{3,1,2,0:T(8,128)S(1)}, f32[1,6,1,8192]{3,1,2,0:T(8,128)S(1)}, u32[]{:S(2)}, u32[]{:S(2)}) collective-permute-start(f32[1,6,1,8192]{3,1,2,0:T(8,128)S(1)} %get-tuple-element.12), channel_id=1, source_target_pairs={{1,0},{2,1},{3,2},{4,3},{5,4},{6,5},{7,6},{8,7},{9,8},{10,9},{11,1... | collective-permute-start | bytes 589832 | tf_op jit(solution)/shard_map/ppermute | solution.py:19
  14.3 268.0 %collective-permute-start.1 = (f32[1,6,1,8192]{3,1,2,0:T(8,128)S(1)}, f32[1,6,1,8192]{3,1,2,0:T(8,128)S(1)}, u32[]{:S(2)}, u32[]{:S(2)}) collective-permute-start(f32[1,6,1,8192]{3,1,2,0:T(8,128)S(1)} %get-tuple-element.13), channel_id=1, source_target_pairs={{0,1},{1,2},{2,3},{3,4},{4,5},{5,6},{6,7},{7,8},{8,9},{9,10},{10,1... | collective-permute-start | bytes 589832 | tf_op jit(solution)/shard_map/ppermute | solution.py:18
  260.0 22.3 %copy-start.2 = (f32[1,6,8,8192]{3,2,1,0:T(8,128)S(1)}, f32[1,6,8,8192]{3,2,1,0:T(8,128)}, u32[]{:S(2)}) copy-start(f32[1,6,8,8192]{3,2,1,0:T(8,128)} %param.9) | copy-start | bytes 4718596
  260.0 22.4 %copy-start.4 = (f32[1,6,8,8192]{3,1,2,0:T(8,128)S(1)}, f32[1,6,8,8192]{3,1,2,0:T(8,128)}, u32[]{:S(2)}) copy-start(f32[1,6,8,8192]{3,1,2,0:T(8,128)} %copy-done.3) | copy-start | bytes 4718596
  260.0 22.4 %copy-start.8 = (f32[1,6,8,8192]{3,2,1,0:T(8,128)S(1)}, f32[1,6,8,8192]{3,2,1,0:T(8,128)}, u32[]{:S(2)}) copy-start(f32[1,6,8,8192]{3,2,1,0:T(8,128)} %param.13) | copy-start | bytes 4718596
  287.5 2.1 copy-start.13
  289.5 5.4 copy-start.16
  289.5 5.5 copy-start.19
  289.5 22.6 %copy-start.12 = (f32[1,18,2048]{2,0,1:T(1,128)S(1)}, f32[1,18,2048]{2,0,1:T(1,128)}, u32[]{:S(2)}) copy-start(f32[1,18,2048]{2,0,1:T(1,128)} %param.14) | copy-start | bytes 442372
  304.0 300.8 %all-to-all-start = ((s32[1,16,256]{2,0,1:T(1,128)}), s32[1,16,256]{2,0,1:T(1,128)S(1)}, u32[]{:S(2)}, u32[]{:S(2)}) async-start(s32[1,16,256]{2,0,1:T(1,128)} %bitcast.24), calls=%async_computation | async-start | bytes 32768 | tf_op jit(solution)/shard_map/all_to_all | solution.py:100
  312.5 3.2 copy-start.18
  312.5 3.3 copy-start.17
  312.6 3.4 copy-start.15
  312.6 3.4 copy-start.11
  312.6 3.4 copy-start.14
  318.1 1.3 copy-start.5
  320.1 247.2 %collective-permute-start.2 = (f32[1,6,1,8192]{3,1,2,0:T(8,128)}, f32[1,6,1,8192]{3,1,2,0:T(8,128)S(1)}, u32[]{:S(2)}, u32[]{:S(2)}) collective-permute-start(f32[1,6,1,8192]{3,1,2,0:T(8,128)} %get-tuple-element.10), channel_id=1, source_target_pairs={{1,0},{2,1},{3,2},{4,3},{5,4},{6,5},{7,6},{8,7},{9,8},{10,9},{11,1... | collective-permute-start | bytes 589832 | tf_op jit(solution)/shard_map/ppermute | solution.py:19
  320.4 246.8 %collective-permute-start.3 = (f32[1,6,1,8192]{3,1,2,0:T(8,128)S(1)}, f32[1,6,1,8192]{3,1,2,0:T(8,128)S(1)}, u32[]{:S(2)}, u32[]{:S(2)}) collective-permute-start(f32[1,6,1,8192]{3,1,2,0:T(8,128)S(1)} %get-tuple-element.11), channel_id=1, source_target_pairs={{0,1},{1,2},{2,3},{3,4},{4,5},{5,6},{6,7},{7,8},{8,9},{9,10},{10,1... | collective-permute-start | bytes 589832 | tf_op jit(solution)/shard_map/ppermute | solution.py:18
  544.8 22.5 %copy-start.6 = (f32[1,6,8,8192]{3,1,2,0:T(8,128)S(1)}, f32[1,6,8,8192]{3,1,2,0:T(8,128)}, u32[]{:S(2)}) copy-start(f32[1,6,8,8192]{3,1,2,0:T(8,128)} %copy-done.5) | copy-start | bytes 4718596
  544.8 22.5 %copy-start.9 = (f32[1,6,8,8192]{3,2,1,0:T(8,128)S(1)}, f32[1,6,8,8192]{3,2,1,0:T(8,128)}, u32[]{:S(2)}) copy-start(f32[1,6,8,8192]{3,2,1,0:T(8,128)} %param.13) | copy-start | bytes 4718596
  604.8 31.2 %all-to-all-start.1 = ((f32[3,16,256]{2,0,1:T(4,128)}), f32[3,16,256]{2,0,1:T(4,128)S(1)}, u32[]{:S(2)}, u32[]{:S(2)}) async-start(f32[3,16,256]{2,0,1:T(4,128)} %copy.54), calls=%async_computation.1 | async-start | bytes 131072 | tf_op jit(solution)/shard_map/all_to_all | solution.py:99
  636.0 40.4 %all-to-all-start.2 = ((f32[3,16,256]{2,0,1:T(4,128)}), f32[3,16,256]{2,0,1:T(4,128)S(1)}, u32[]{:S(2)}, u32[]{:S(2)}) async-start(f32[3,16,256]{2,0,1:T(4,128)} %copy.57), calls=%async_computation.2 | async-start | bytes 131072 | tf_op jit(solution)/shard_map/all_to_all | solution.py:99
  643.6 30.8 %copy-start = (f32[1,6,8,8192]{3,1,2,0:T(8,128)S(1)}, f32[1,6,8,8192]{3,1,2,0:T(8,128)}, u32[]{:S(2)}) copy-start(f32[1,6,8,8192]{3,1,2,0:T(8,128)} %fusion.8) | copy-start | bytes 4718596
  676.4 30.7 %copy-start.7 = (f32[4096,3]{1,0:T(8,128)S(1)}, f32[4096,3]{1,0:T(8,128)}, u32[]{:S(2)}) copy-start(f32[4096,3]{1,0:T(8,128)} %scatter_custom_fusion) | copy-start | bytes 147460
Sparse Core Ops, SparseCore 0:
  9.7 250.3 all-gather.4
  289.7 255.0 all-gather.6
